TPU v7x, 512 devices: a whole 4x8x8 slice. The times are simulated.
512 devices in a mesh: row: 32 (over z_hi, y, core), col: 16 (over x, z_lo).
Axes of the slice: x: 4, y: 8, z: 8 (z_hi: 2, z_lo: 4; z = z_hi * 4 + z_lo), core: 2. Of those that a mesh axis runs over, the one named last changes fastest.
Arguments:
- matrix: float32 [16384, 16384], P('row', 'col'), as said below
- lower_inverse: float32 [256, 256], replicated, as said below
- rhs: float32 [16384, 512], P('row', 'col'), may hold values from -6 to 6
- sources: int32 [512], P('col'), may hold values from 0 to 16383
Outputs:
- updated: float32 [16384, 16384], P('row', 'col')
- rhs_out: float32 [16384, 512], P('row', 'col')
Inputs may be any that keep to these rules, and one draw needn't show every extreme that they name: matrix is exactly symmetric. lower_inverse is lower triangular with a positive diagonal; it is drawn independently of matrix and need not be the inverse factor of matrix's diagonal block.
All inputs are finite; a program needn't handle non-finite values.
Results may differ from a plain program's by a relative error of at most 0.00005.
Values sent between devices are 32-bit elements; how exact they have to be, the bound alone decides.
A program may use at most 64 MiB of HBM per device.

v0:
```python
import functools

import jax
import jax.numpy as jnp
from jax import lax
from jax.experimental import pallas as pl
from jax.experimental.pallas import tpu as pltpu
from jax.sharding import PartitionSpec as P

MESH = pl.DeviceIdType.MESH
NY = 8
NX = 4
NL = 4
NT = ((1,), (1,))
NN = ((1,), (0,))


def coords():
    r = lax.axis_index("row")
    q = lax.axis_index("col")
    return r // 16, (r // 2) % NY, r % 2, q // NL, q % NL


def device(h, y, c, x, l):
    return (h * 16 + y * 2 + c, x * NL + l)


def remote(src, dst, send, recv, target):
    return pltpu.make_async_remote_copy(
        src_ref=src,
        dst_ref=dst,
        send_sem=send,
        recv_sem=recv,
        device_id=device(*target),
        device_id_type=MESH,
    )


def halves(value):
    high = value.astype(jnp.bfloat16)
    return high, (value - high.astype(jnp.float32)).astype(jnp.bfloat16)


def dot3(a, b, contract):
    (ah, al), (bh, bl) = a, b

    def one(u, v):
        return lax.dot_general(u, v, (contract, ((), ())), preferred_element_type=jnp.float32)

    return one(ah, bh) + (one(ah, bl) + one(al, bh))


def spread_kernel(
    matrix, rhs_t, inverse,
    factor, factor_hi, factor_lo, wide_hi, wide_lo, inv_hi, inv_lo, top_rhs,
    left, top, inv,
    t1_send, t_send, s_send, p1_send, p_send,
    t_recv, s_recv, p_recv, local_sem, ready, ready_top, ready_left,
):
    h, y, c, x, l = coords()
    s = 1 - 2 * c
    top_root = (h == 0) & (y == 0) & (c == 0)
    left_root = (x == 0) & (l == 0)
    no = jnp.logical_not
    on = pl.when

    def yy(k):
        return lax.rem(y + k + 2 * NY, NY)

    def xx(k):
        return lax.rem(x + k, NX)

    def ll(k):
        return lax.rem(l + k, NL)

    load_inverse = pltpu.make_async_copy(inverse, inv, local_sem.at[0])
    load_left = pltpu.make_async_copy(matrix.at[:, pl.ds(0, 256)], left, local_sem.at[1])

    @on(top_root)
    def _():
        for a in range(NY):
            for b in range(2):
                pltpu.make_async_copy(
                    matrix.at[pl.ds(b * 128, 128), pl.ds(a * 128, 128)],
                    top.at[a, b, pl.ds(0, 128)], local_sem.at[2],
                ).start()
                pltpu.make_async_copy(
                    rhs_t.at[pl.ds((a // 2) * 8, 8), pl.ds((a % 2) * 128, 128)],
                    top.at[a, b, pl.ds(128, 8)], local_sem.at[2],
                ).start()

    @on(left_root)
    def _():
        load_left.start()

    load_inverse.start()

    barrier = pltpu.get_barrier_semaphore()

    def signal(semaphore, target):
        pl.semaphore_signal(semaphore, inc=1, device_id=device(*target), device_id_type=MESH)

    def rank(v, n):
        return jnp.minimum(v, n - v) * n + v

    partners = []
    for k, slot, back in ((2, 2, 3), (-2, 3, 2), (1, 0, 1), (-1, 1, 0)):
        partners.append((slot, back, (h, yy(k), c, x, l), rank(y, NY) < rank(yy(k), NY)))
    partners.append((10, 10, (1 - h, y, c, x, l), h == 0))
    for k, slot, back in ((2, 8, 8), (1, 7, 9), (3, 9, 7)):
        partners.append((slot, back, (h, y, c, x, ll(k)), l < ll(k)))
    for k, slot, back in ((2, 5, 5), (1, 4, 6), (3, 6, 4)):
        partners.append((slot, back, (h, y, c, xx(k), l), rank(x, NX) < rank(xx(k), NX)))
    partners.append((11, 11, (h, y, 1 - c, x, l), c == 0))
    def is_last(target):
        return sum(target) == 0

    last = is_last((h, y, c, x, l))
    partners = [
        (slot, back, target, no(last) & (early | is_last(target)) if slot in (0, 1, 2, 3, 11) else early)
        for slot, back, target, early in partners
    ]
    earlier = {slot: early for slot, _, _, early in partners}

    near = jnp.minimum(y, NY - y)
    far_top = (h == 0) & (((c == 1) & (y > 0)) | ((c == 0) & (near > 2)))
    far_left = (x > 0) & (l > 0)

    top_last = is_last((0, 0, 0, x, l))

    @on(far_top & top_last)
    def _():
        signal(barrier, (0, 0, 0, x, l))

    @on(top_root & no(last))
    def _():
        for a in (1, 7, 2, 6, 3, 5, 4):
            signal(barrier, (0, a, 1, x, l))
        for a in (3, 5, 4):
            signal(barrier, (0, a, 0, x, l))

    @on(left_root)
    def _():
        for a in range(1, NX):
            for b in range(1, NL):
                signal(barrier, (h, y, c, a, b))

    expected = (
        jnp.where(far_top & no(top_last), 1, 0)
        + jnp.where(far_left, 1, 0)
        + jnp.where(last, 10, 0)
    )
    for slot, back, target, early in partners:
        expected = expected + jnp.where(early, 0, 1)

        @on(early)
        def _():
            signal(barrier, target)

    def settle(who):
        @on(who & (expected > 0))
        def _():
            pl.semaphore_wait(barrier, expected)

        @on(who & far_top & no(top_last))
        def _():
            signal(ready_top.at[y], (0, 0, 0, x, l))

        @on(who & far_left)
        def _():
            signal(ready_left.at[x * NL + l], (h, y, c, 0, 0))

        for slot, back, target, early in partners:
            @on(who & no(early))
            def _():
                signal(ready.at[back], target)

    first_root = top_root & no(last)
    settle(no(first_root))

    def need(slot):
        @on(earlier[slot])
        def _():
            pl.semaphore_wait(ready.at[slot], 1)

    def piece(a, b):
        return left.at[pl.ds(pl.multiple_of(a * 128 + b * 32, 32), 32)]

    def left_scatter(a, b):
        return remote(
            piece(a, b), piece(a, b), p1_send.at[a * NL + b], p_recv.at[a * NL + b], (h, y, c, a, b)
        )

    def left_copy(a, b, j, target):
        return remote(piece(a, b), piece(a, b), p_send.at[j], p_recv.at[a * NL + b], target)

    def left_wait(a, b):
        @on(no(left_root))
        def _():
            left_copy(a, b, 0, (h, y, c, x, l)).wait_recv()

    def top_scatter(a, b):
        return remote(
            top.at[a, b], top.at[a, b], t1_send.at[a * 2 + b], t_recv.at[a], (0, a, b, x, l)
        )

    def top_beside(a):
        return remote(
            top.at[a, 1], top.at[a, 1], t1_send.at[16 + a], t_recv.at[a], (0, 0, 1, x, l)
        )

    def top_copy(a, j, target):
        return remote(top.at[a, c], top.at[a, c], t_send.at[j], t_recv.at[a], target)

    def top_wait(a):
        @on(no(top_root))
        def _():
            top_copy(a, 0, (h, y, c, x, l)).wait_recv()

    def has_all(k):
        return (h == 0) & (yy(k) == 0)

    def top_send(a, j, k):
        @on(no(has_all(k)))
        def _():
            top_copy(a, j, (h, yy(k), c, x, l)).start()

    def sibling(a, half):
        return remote(
            top.at[a, half], top.at[a, half], s_send.at[a], s_recv.at[a], (h, y, 1 - c, x, l)
        )

    beside_root = (h == 0) & (y == 0) & (c == 1)

    def sibling_send(a):
        @on(no(beside_root))
        def _():
            sibling(a, c).start()

    def top_pair(a, slot):
        if slot is not None:
            need(slot)

        @on(no(last))
        def _():
            pl.semaphore_wait(ready_top.at[a], 2 if slot is None else 1)

        for b in range(2):
            top_scatter(a, b).start()

    left_order = [
        (1, 0), (3, 0), (0, 1), (2, 0), (1, 1), (3, 1), (0, 2), (2, 1),
        (1, 2), (3, 2), (0, 3), (2, 2), (1, 3), (3, 3), (2, 3),
    ]

    @on(top_root)
    def _():
        pltpu.make_async_copy(top, top, local_sem.at[2]).wait()
        top_pair(1, 0)
        top_pair(7, 1)
        top_pair(2, 2)
        top_pair(6, 3)
        top_pair(3, None)
        top_pair(5, None)
        top_pair(4, None)
        need(11)
        top_scatter(0, 1).start()
        for a in (6, 2, 1, 7, 3, 5, 4):
            top_beside(a).start()

    settle(first_root)

    @on(left_root)
    def _():
        load_left.wait()
        for a, b in left_order:
            if b == 0:
                need({1: 4, 2: 5, 3: 6}[a])
            elif a == 0:
                need({1: 7, 2: 8, 3: 9}[b])
            else:
                pl.semaphore_wait(ready_left.at[a * NL + b], 1)
            left_scatter(a, b).start()

    load_inverse.wait()
    high, low = halves(inv[...])
    inv_hi[...] = high
    inv_lo[...] = low

    def own_left():
        left_wait(x, l)

        @on(no(left_root))
        def _():
            for slot in (8, 7, 9, 5, 4, 6):
                need(slot)

        for k in (2, 1, 3):
            @on(no((x == 0) & (ll(k) == 0)))
            def _():
                left_copy(x, l, k - 1, (h, y, c, x, ll(k))).start()
        for k in (2, 1, 3):
            @on(no((l == 0) & (xx(k) == 0)))
            def _():
                left_copy(x, l, 2 + k, (h, y, c, xx(k), l)).start()

    def own_top():
        top_wait(y)

        @on(no(top_root))
        def _():
            for slot in (2, 3, 0, 1, 11):
                need(slot)

        for k in (2, -2, 1, -1):
            top_send(y, 3 + k, k)

        @on(h == 0)
        def _():
            need(10)
            top_copy(y, 10, (1, y, c, x, l)).start()

        sibling_send(y)

    def left_relay(m):
        left_wait(x, ll(m))
        for k in (2, 1, 3):
            @on(no((l == 0) & (xx(k) == 0)))
            def _():
                left_copy(x, ll(m), 3 * m + 2 + k, (h, y, c, xx(k), l)).start()

    ahead = yy(-2 * s)
    behind = yy(2 * s)

    def relay_ahead():
        top_wait(ahead)
        top_send(ahead, 3, 2 * s)
        top_send(ahead, 8, s)
        sibling_send(ahead)

    def relay_behind():
        top_wait(behind)
        top_send(behind, 9, -s)
        sibling_send(behind)

    def top_tail(k):
        top_wait(yy(k))
        sibling_send(yy(k))

    inv_halves = (inv_hi[...], inv_lo[...])

    def block(i):
        rows = pl.ds(pl.multiple_of(i * 128, 128), 128)
        part = dot3(halves(left[rows, :]), inv_halves, NT)
        factor[rows, :] = part
        high, low = halves(part)
        factor_hi[rows, :] = high
        factor_lo[rows, :] = low

    def others(k):
        for b in range(NL):
            left_wait(xx(k), b)
        block(xx(k))

    def broad(k):
        a = yy(k)

        @on(no(top_root))
        def _():
            sibling(a, 1 - c).wait_recv()

        chunk = jnp.concatenate([top[a, b, pl.ds(0, 128), :] for b in range(2)], axis=0)
        high, low = halves(dot3(inv_halves, halves(chunk), NN))
        wide_hi[a] = high
        wide_lo[a] = low
        top_rhs[a] = top[a, 0, pl.ds(128, 8), :]

    own_left()
    own_top()
    for m in (1, 3, 2):
        left_relay(m)
    relay_ahead()
    relay_behind()
    block(x)
    top_tail(1)
    top_tail(-1)
    others(1)
    top_tail(3)
    others(3)
    top_tail(-3)
    others(2)
    broad(0)
    top_tail(4)
    for k in (2, -2, 1, -1, 3, -3, 4):
        broad(k)

    for k in (1, 2, 3):
        @on(no((x == 0) & (ll(k) == 0)))
        def _():
            left_copy(x, l, k - 1, (h, y, c, x, l)).wait_send()

        @on(no((l == 0) & (xx(k) == 0)))
        def _():
            for m in range(NL):
                left_copy(x, l, 3 * m + 2 + k, (h, y, c, x, l)).wait_send()

    for j, k in ((1, -2), (2, -1), (4, 1), (5, 2), (3, 2 * s), (8, s), (9, -s)):
        @on(no(has_all(k)))
        def _():
            top_copy(y, j, (h, y, c, x, l)).wait_send()

    @on(no(beside_root))
    def _():
        for a in range(NY):
            sibling(a, c).wait_send()

    @on(h == 0)
    def _():
        top_copy(y, 10, (h, y, c, x, l)).wait_send()

    @on(left_root)
    def _():
        for a, b in left_order:
            left_scatter(a, b).wait_send()

    @on(top_root)
    def _():
        top_scatter(0, 1).wait_send()
        for a in range(1, NY):
            top_beside(a).wait_send()
            for b in range(2):
                top_scatter(a, b).wait_send()


def spread(matrix, rhs_t, inverse, sources=None):
    hbm = lambda value: pltpu.with_memory_space_constraint(value, pltpu.HBM)
    dma = pltpu.SemaphoreType.DMA
    regular = pltpu.SemaphoreType.REGULAR
    f32 = jnp.float32
    b16 = jnp.bfloat16
    return pl.pallas_call(
        spread_kernel,
        out_shape=(
            jax.ShapeDtypeStruct((512, 256), f32),
            jax.ShapeDtypeStruct((512, 256), b16),
            jax.ShapeDtypeStruct((512, 256), b16),
            jax.ShapeDtypeStruct((NY, 256, 128), b16),
            jax.ShapeDtypeStruct((NY, 256, 128), b16),
            jax.ShapeDtypeStruct((256, 256), b16),
            jax.ShapeDtypeStruct((256, 256), b16),
            jax.ShapeDtypeStruct((NY, 8, 128), f32),
        ),
        in_specs=[pl.BlockSpec(memory_space=pltpu.HBM)] * 3,
        out_specs=(pl.BlockSpec(memory_space=pltpu.VMEM),) * 8,
        scratch_shapes=[
            pltpu.VMEM((512, 256), f32),
            pltpu.VMEM((NY, 2, 136, 128), f32),
            pltpu.VMEM((256, 256), f32),
            dma((24,)), dma((11,)), dma((8,)), dma((16,)), dma((15,)),
            dma((8,)), dma((8,)), dma((16,)), dma((3,)),
            regular((12,)), regular((8,)), regular((16,)),
        ],
        compiler_params=pltpu.CompilerParams(
            collective_id=0, has_side_effects=True, vmem_limit_bytes=24 << 20
        ),
        name="spread_panel",
    )(hbm(matrix), hbm(rhs_t), hbm(inverse))


def update_kernel(
    factor, factor_hi, factor_lo, wide_hi, wide_lo, inv_hi, inv_lo, top_rhs,
    matrix, rhs_t, sources, updated, rhs_out, result, out_sem,
):
    row_index = lax.axis_index("row")
    col_index = lax.axis_index("col")
    wide = tuple(
        jnp.concatenate([ref[i] for i in range(NY)], axis=1) for ref in (wide_hi, wide_lo)
    )
    copies = []
    for i in range(NX):
        rows = pl.ds(i * 128, 128)
        product = dot3((factor_hi[rows, :], factor_lo[rows, :]), wide, NN)
        held = matrix[rows, :]
        result[rows, :] = held - product

        @pl.when(col_index == 0)
        def _():
            result[rows, pl.ds(0, 256)] = factor[rows, :]

        if i < 2:
            @pl.when(row_index == 0)
            def _():
                result[rows, :] = held

        copy = pltpu.make_async_copy(result.at[rows], updated.at[rows], out_sem.at[i])
        copy.start()
        copies.append(copy)

    spare = jnp.broadcast_to(sources[...].astype(jnp.float32), (32, 32))
    eye = lax.broadcasted_iota(jnp.int32, (32, 32), 0) == lax.broadcasted_iota(jnp.int32, (32, 32), 1)
    column = jnp.sum(jnp.where(eye, spare, 0.0), axis=1, keepdims=True).astype(jnp.int32)
    ids = lax.broadcasted_iota(jnp.int32, (32, 512), 1)
    driven = rhs_t[...] + jnp.where(ids + row_index * 512 == column, 1.0, 0.0)
    first = jnp.concatenate(
        [jnp.concatenate([top_rhs[2 * i], top_rhs[2 * i + 1]], axis=1) for i in range(4)], axis=0
    )
    first = first + jnp.where(ids[:, :256] == column, 1.0, 0.0)
    solve = dot3(halves(first), (inv_hi[...], inv_lo[...]), NT)
    rest = driven - dot3(halves(solve), (factor_hi[...], factor_lo[...]), NT)
    rhs_out[...] = rest

    @pl.when(row_index == 0)
    def _():
        rhs_out[:, pl.ds(0, 256)] = solve

    for copy in copies:
        copy.wait()


def update(parts, matrix, rhs_t, sources):
    vmem = pl.BlockSpec(memory_space=pltpu.VMEM)
    return pl.pallas_call(
        update_kernel,
        out_shape=(
            jax.ShapeDtypeStruct((512, 1024), jnp.float32),
            jax.ShapeDtypeStruct((32, 512), jnp.float32),
        ),
        in_specs=[vmem] * 11,
        out_specs=(pl.BlockSpec(memory_space=pl.ANY), vmem),
        scratch_shapes=[pltpu.VMEM((512, 1024), jnp.float32), pltpu.SemaphoreType.DMA((NX,))],
        compiler_params=pltpu.CompilerParams(vmem_limit_bytes=24 << 20),
        name="update_trailing",
    )(*parts, matrix, rhs_t, sources)


def shards(matrix, lower_inverse, rhs, sources):
    rhs_t = rhs.T
    parts = spread(matrix, rhs_t, lower_inverse)
    updated, rhs_out = update(parts, matrix, rhs_t, sources.reshape(1, -1))
    return updated, rhs_out.T


def solution(mesh):
    placed = (P("row", "col"), P(), P("row", "col"), P("col"))
    return jax.shard_map(
        shards,
        mesh=mesh,
        in_specs=placed,
        out_specs=(P("row", "col"), P("row", "col")),
        check_vma=False,
    )
```

profile of v0, /device:TPU:2, one launch (start us, length us, event | category | flops | bytes accessed | tf_op | source)
XLA Modules:
  0.0 37.7 jit_solution(9318856910532744714)
XLA Ops:
  0.6 0.0 copy-start
  0.6 0.0 copy-start.2
  0.7 0.0 copy-start.1
  0.7 33.9 %spread_panel.1 = (f32[512,256]{1,0:T(8,128)S(1)}, bf16[512,256]{1,0:T(8,128)(2,1)S(1)}, bf16[512,256]{1,0:T(8,128)(2,1)S(1)}, bf16[8,256,128]{2,1,0:T(8,128)(2,...) custom-call(f32[512,1024]{1,0:T(8,128)} %matrix.3, ...), custom_call_target="tpu_custom_call" | custom-call | tf_op jit(solution)/shard_map/spread_panel/pallas_call | solution.py:441
  34.6 0.0 copy-done
  34.6 0.0 copy-done.2
  34.6 0.0 copy-done.1
  34.6 3.1 %update_trailing.1 = (f32[512,1024]{1,0:T(8,128)}, f32[32,512]{1,0:T(8,128)}) custom-call(f32[512,256]{1,0:T(8,128)S(1)} %get-tuple-element.12.factor, bf16[512,256]{1,0:T(8,128)(2,1)S(1)} %get-tuple-element.13.factor_hi, bf16[512,256]{1,0:T(8,128)(2,1)S(1)} %get-tuple-element.14.factor_lo, bf16[8,256,128]{2,1,0:T(8,128)(2,1)S(1)} %get-tuple-element.15.wide_hi, ...), custom_call_target="tpu_custom_call" | custom-call | tf_op jit(solution)/shard_map/update_trailing/pallas_call | solution.py:522
Async XLA Ops:
  0.6 34.0 %copy-start = (f32[512,1024]{1,0:T(8,128)S(1)}, f32[512,1024]{1,0:T(8,128)}, u32[]{:S(2)}) copy-start(f32[512,1024]{1,0:T(8,128)} %matrix.3) | copy-start | bytes 6291460
  0.6 34.0 %copy-start.2 = (s32[32]{0:T(128)S(1)}, s32[32]{0:T(128)}, u32[]{:S(2)}) copy-start(s32[32]{0:T(128)} %param.7) | copy-start | bytes 388
  0.7 34.0 %copy-start.1 = (f32[512,32]{0,1:T(8,128)S(1)}, f32[512,32]{0,1:T(8,128)}, u32[]{:S(2)}) copy-start(f32[512,32]{0,1:T(8,128)} %param.6) | copy-start | bytes 196612
where the time goes:
time: 37.9 us; the launch traced here: 37.7 us
  Pallas kernels  37 us (98%)
  between operations  0.69 us (2%)
    pallas_call x1, Pallas kernels, spread(): pl.pallas_call(spread_kernel, out_shape=(jax.ShapeDtypeStruct((512, 256),...  33.9 us
    pallas_call x1, Pallas kernels, update(): pl.pallas_call(update_kernel, out_shape=(jax.ShapeDtypeStruct((512, 1024)...  3.09 us

commit v1 on v0

--- a/solution.py
+++ b/solution.py
@@ -230,6 +230,7 @@
             top.at[a, half], top.at[a, half], s_send.at[a], s_recv.at[a], (h, y, 1 - c, x, l)
         )
 
+    root_chip = (h == 0) & (y == 0)
     beside_root = (h == 0) & (y == 0) & (c == 1)
 
     def sibling_send(a):
@@ -312,10 +313,15 @@
             for slot in (2, 3, 0, 1, 11):
                 need(slot)
 
+        @on((h == 0) & no(root_chip))
+        def _():
+            need(10)
+            top_copy(y, 10, (1, y, c, x, l)).start()
+
         for k in (2, -2, 1, -1):
             top_send(y, 3 + k, k)
 
-        @on(h == 0)
+        @on(root_chip)
         def _():
             need(10)
             top_copy(y, 10, (1, y, c, x, l)).start()

time: 37.9 us -> 37.9 us (level)
  no operation moved by 1% of the time
where the time goes in v1:
time: 37.9 us; the launch traced here: 37.7 us
  Pallas kernels  37 us (98%)
  between operations  0.69 us (2%)
    pallas_call x1, Pallas kernels, spread(): pl.pallas_call(spread_kernel, out_shape=(jax.ShapeDtypeStruct((512, 256),...  33.9 us
    pallas_call x1, Pallas kernels, update(): pl.pallas_call(update_kernel, out_shape=(jax.ShapeDtypeStruct((512, 1024)...  3.09 us

profile of v1, /device:TPU:2, one launch (start us, length us, event | category | flops | bytes accessed | tf_op | source)
XLA Modules:
  0.0 37.7 jit_solution(5221004753612910725)
XLA Ops:
  0.6 0.0 copy-start
  0.6 0.0 copy-start.2
  0.7 0.0 copy-start.1
  0.7 33.9 %spread_panel.1 = (f32[512,256]{1,0:T(8,128)S(1)}, bf16[512,256]{1,0:T(8,128)(2,1)S(1)}, bf16[512,256]{1,0:T(8,128)(2,1)S(1)}, bf16[8,256,128]{2,1,0:T(8,128)(2,...) custom-call(f32[512,1024]{1,0:T(8,128)} %matrix.3, ...), custom_call_target="tpu_custom_call" | custom-call | tf_op jit(solution)/shard_map/spread_panel/pallas_call | solution.py:447
  34.6 0.0 copy-done
  34.6 0.0 copy-done.2
  34.6 0.0 copy-done.1
  34.6 3.1 %update_trailing.1 = (f32[512,1024]{1,0:T(8,128)}, f32[32,512]{1,0:T(8,128)}) custom-call(f32[512,256]{1,0:T(8,128)S(1)} %get-tuple-element.12.factor, bf16[512,256]{1,0:T(8,128)(2,1)S(1)} %get-tuple-element.13.factor_hi, bf16[512,256]{1,0:T(8,128)(2,1)S(1)} %get-tuple-element.14.factor_lo, bf16[8,256,128]{2,1,0:T(8,128)(2,1)S(1)} %get-tuple-element.15.wide_hi, ...), custom_call_target="tpu_custom_call" | custom-call | tf_op jit(solution)/shard_map/update_trailing/pallas_call | solution.py:528
Async XLA Ops:
  0.6 34.0 %copy-start = (f32[512,1024]{1,0:T(8,128)S(1)}, f32[512,1024]{1,0:T(8,128)}, u32[]{:S(2)}) copy-start(f32[512,1024]{1,0:T(8,128)} %matrix.3) | copy-start | bytes 6291460
  0.6 34.0 %copy-start.2 = (s32[32]{0:T(128)S(1)}, s32[32]{0:T(128)}, u32[]{:S(2)}) copy-start(s32[32]{0:T(128)} %param.7) | copy-start | bytes 388
  0.7 34.0 %copy-start.1 = (f32[512,32]{0,1:T(8,128)S(1)}, f32[512,32]{0,1:T(8,128)}, u32[]{:S(2)}) copy-start(f32[512,32]{0,1:T(8,128)} %param.6) | copy-start | bytes 196612
